TPU v7x, 32 devices: a whole 2x2x4 slice. The times are simulated.
32 devices in a mesh: grp: 16 (over z, y, x), mem: 2 (over core).
Axes of the slice: x: 2, y: 2, z: 4, core: 2. Of those that a mesh axis runs over, the one named last changes fastest.
Arguments:
- raw_traces: float32 [256, 6030], P(('grp', 'mem')), may hold values from -6 to 6
Outputs:
- correlations: bfloat16 [256, 32, 401], P(('grp', 'mem'))
All inputs are finite; a program needn't handle non-finite values.
Results may differ from a plain program's by a relative error of at most 0.0063.
Values may be sent and summed in bfloat16 or wider, within the bound.
A program may use at most 64 MiB of HBM per device.

v0:
```python
import functools
import math

import jax
import jax.numpy as jnp
import numpy as np
from jax import lax
from jax.experimental import pallas as pl
from jax.experimental.pallas import tpu as pltpu
from jax.sharding import PartitionSpec as P

WINDOWS = 2
WLEN = 1500
NFREQ = 384
TAPS = 32
MAXLAG = 200
LANES = 128
BLOCKS = -(-WLEN // LANES)
REACH = 3 * LANES
SPAN = 2 * LANES * (BLOCKS - 1) + REACH
MESH = pl.DeviceIdType.MESH


def filter_table():
    k = np.arange(TAPS)
    window = 0.5 - 0.5 * np.cos(2.0 * np.pi * (k + 0.5) / TAPS)
    taps = 0.5 * np.sinc((k - (TAPS - 1) / 2.0) * 0.5) * window
    table = np.zeros((REACH, LANES))
    for n in range(LANES):
        table[2 * n : 2 * n + TAPS, n] = taps
    return table.astype(np.float32)


def forward_table():
    phase = np.arange(WLEN)[:, None] * np.arange(1, NFREQ + 1)[None, :] % WLEN
    angle = 2.0 * np.pi * phase / WLEN
    table = np.zeros((BLOCKS * LANES, 2 * NFREQ))
    table[:WLEN] = np.concatenate([np.cos(angle), -np.sin(angle)], axis=1)
    high = table.astype(jnp.bfloat16)
    return np.stack([high, (table - high.astype(np.float64)).astype(jnp.bfloat16)])


def inverse_table():
    shifts = np.arange(2 * MAXLAG + 1) - MAXLAG
    phase = np.mod(np.arange(1, NFREQ + 1)[:, None] * shifts[None, :], WLEN)
    angle = 2.0 * np.pi * phase / WLEN
    return np.concatenate([np.cos(angle), -np.sin(angle)], axis=0).astype(jnp.bfloat16)


def kernel(groups, members, raw_ref, filt_ref, fwd_ref, inv_ref, out_ref,
           padded, blocks, gathered, cross, send_sem, recv_sem):
    count = groups * members
    grp, mem = lax.axis_index("grp"), lax.axis_index("mem")
    me = grp * members + mem
    channels, length = raw_ref.shape
    lags = inv_ref.shape[1]

    barrier = pltpu.get_barrier_semaphore()

    def greet(step, carry):
        peer = lax.rem(me + step, count)
        pl.semaphore_signal(barrier, inc=1, device_id=(peer // members, lax.rem(peer, members)),
                            device_id_type=MESH)
        return carry

    lax.fori_loop(1, count, greet, 0)

    whole = length // LANES * LANES
    padded[:, whole:] = jnp.zeros((channels, padded.shape[1] - whole), jnp.float32)
    padded[:, :length] = raw_ref[...]
    for w in range(WINDOWS):
        start = 2 * WLEN * w
        base = start // LANES * LANES
        if start == base:
            piece = padded[:, start : start + SPAN]
        else:
            width = SPAN + LANES
            piece = pltpu.roll(padded[:, base : base + width], width - (start - base), 1)
        for b in range(BLOCKS):
            row = (w * BLOCKS + b) * channels
            blocks[row : row + channels, :] = piece[:, 2 * LANES * b : 2 * LANES * b + REACH]
    decimated = jnp.dot(blocks[...], filt_ref[...], precision=lax.Precision.HIGHEST,
                        preferred_element_type=jnp.float32)
    frames = jnp.concatenate(
        [
            jnp.concatenate(
                [
                    decimated[(w * BLOCKS + b) * channels : (w * BLOCKS + b + 1) * channels, :]
                    for b in range(BLOCKS)
                ],
                axis=1,
            )
            for w in range(WINDOWS)
        ],
        axis=0,
    )
    rows = WINDOWS * channels
    high = frames.astype(jnp.bfloat16)
    low = (frames - high.astype(jnp.float32)).astype(jnp.bfloat16)
    parts = jnp.dot(jnp.concatenate([high, low], axis=0), fwd_ref[0],
                    preferred_element_type=jnp.float32)
    spec = parts[:rows] + parts[rows:]
    spec = spec + jnp.dot(high, fwd_ref[1], preferred_element_type=jnp.float32)
    spec_re, spec_im = spec[:, :NFREQ], spec[:, NFREQ:]
    power = spec_re * spec_re + spec_im * spec_im
    level = 0.01 * jnp.mean(power, axis=1, keepdims=True)
    factor = 1.0 / jnp.sqrt(power + level + 1e-06)
    white = jnp.concatenate([spec_re * factor, spec_im * factor], axis=1)
    own = white.astype(jnp.bfloat16).astype(jnp.float32)
    gathered[me] = jnp.concatenate(
        [own[w * channels : w * channels + 1] for w in range(WINDOWS)], axis=0
    ).astype(jnp.bfloat16)

    pl.semaphore_wait(barrier, count - 1)

    def send(step, carry):
        peer = lax.rem(me + step, count)
        pltpu.make_async_remote_copy(
            src_ref=gathered.at[me],
            dst_ref=gathered.at[me],
            send_sem=send_sem,
            recv_sem=recv_sem,
            device_id=(peer // members, lax.rem(peer, members)),
            device_id_type=MESH,
        ).start()
        return carry

    lax.fori_loop(1, count, send, 0)
    others = gathered.at[pl.ds(0, count - 1)]
    pltpu.make_async_copy(others, others, recv_sem).wait()

    panel = min(count, 32)
    size = panel * channels
    to = lax.broadcasted_iota(jnp.int32, (size, size), 0)
    at = lax.broadcasted_iota(jnp.int32, (size, size), 1)
    order = (lax.rem(to, panel) * channels + to // panel == at).astype(jnp.float32).astype(jnp.bfloat16)
    scale = 1.0 / math.sqrt(WINDOWS * NFREQ)

    def work(index, carry):
        for j in range(panel):
            source = gathered[index * panel + j].astype(jnp.float32)
            cross_re = jnp.zeros((channels, NFREQ), jnp.float32)
            cross_im = jnp.zeros((channels, NFREQ), jnp.float32)
            for w in range(WINDOWS):
                a_re = own[w * channels : (w + 1) * channels, :NFREQ]
                a_im = own[w * channels : (w + 1) * channels, NFREQ:]
                b_re = source[w : w + 1, :NFREQ]
                b_im = source[w : w + 1, NFREQ:]
                cross_re = cross_re + (a_re * b_re + a_im * b_im)
                cross_im = cross_im + (a_im * b_re - a_re * b_im)
            cross[j * channels : (j + 1) * channels, :NFREQ] = cross_re
            cross[j * channels : (j + 1) * channels, NFREQ:] = cross_im
        turned = jnp.dot(order, cross[...].astype(jnp.bfloat16),
                         preferred_element_type=jnp.float32).astype(jnp.bfloat16)
        corr = jnp.dot(turned, inv_ref[...], preferred_element_type=jnp.float32) * scale
        corr = corr.astype(jnp.bfloat16)
        for c in range(channels):
            out_ref[c, pl.ds(pl.multiple_of(index * panel, panel), panel), :] = corr[c * panel : (c + 1) * panel]
        return carry

    if count == panel:
        work(0, 0)
    else:
        lax.fori_loop(0, count // panel, work, 0)
    pltpu.make_async_copy(others, others, send_sem).wait()


def solution(mesh):
    groups, members = mesh.shape["grp"], mesh.shape["mem"]
    count = groups * members
    filt, fwd, inv = filter_table(), forward_table(), inverse_table()

    def on_device(raw_traces):
        channels, length = raw_traces.shape
        start = 2 * WLEN * (WINDOWS - 1) // LANES * LANES
        return pl.pallas_call(
            functools.partial(kernel, groups, members),
            out_shape=jax.ShapeDtypeStruct((channels, count, inv.shape[1]), jnp.bfloat16),
            in_specs=[pl.BlockSpec(memory_space=pltpu.VMEM)] * 4,
            out_specs=pl.BlockSpec(memory_space=pltpu.VMEM),
            scratch_shapes=[
                pltpu.VMEM((channels, start + SPAN + LANES), jnp.float32),
                pltpu.VMEM((WINDOWS * BLOCKS * channels, REACH), jnp.float32),
                pltpu.VMEM((count, WINDOWS, 2 * NFREQ), jnp.bfloat16),
                pltpu.VMEM((min(count, 32) * channels, 2 * NFREQ), jnp.float32),
                pltpu.SemaphoreType.DMA,
                pltpu.SemaphoreType.DMA,
            ],
            compiler_params=pltpu.CompilerParams(
                collective_id=0, has_side_effects=True, vmem_limit_bytes=48 * 1024 * 1024
            ),
        )(raw_traces, jnp.asarray(filt), jnp.asarray(fwd), jnp.asarray(inv))

    return jax.shard_map(
        on_device,
        mesh=mesh,
        in_specs=(P(("grp", "mem"), None),),
        out_specs=P(("grp", "mem"), None, None),
        check_vma=False,
    )
```

profile of v0, /device:TPU:0, one launch (start us, length us, event | category | flops | bytes accessed | tf_op | source)
XLA Modules:
  0.0 17.2 jit_solution(13663209836824520657)
XLA Ops:
  0.0 0.0 copy-start
  0.0 2.3 %copy-done = bf16[2,1536,768]{2,1,0:T(8,128)(2,1)S(1)} copy-done((bf16[2,1536,768]{2,1,0:T(8,128)(2,1)S(1)}, bf16[2,1536,768]{2,1,0:T(8,128)(2,1)}, u32[]{:S(2)}) %copy-start) | copy-done | bytes 4718616
  2.3 0.0 copy-start.1
  2.3 1.1 %copy-done.1 = bf16[768,401]{1,0:T(8,128)(2,1)S(1)} copy-done((bf16[768,401]{1,0:T(8,128)(2,1)S(1)}, bf16[768,401]{1,0:T(8,128)(2,1)}, u32[]{:S(2)}) %copy-start.1) | copy-done | bytes 615960
  3.5 0.0 copy-start.2
  3.5 0.9 %copy-done.2 = f32[8,6030]{1,0:T(8,128)S(1)} copy-done((f32[8,6030]{1,0:T(8,128)S(1)}, f32[8,6030]{1,0:T(8,128)}, u32[]{:S(2)}) %copy-start.2) | copy-done | bytes 192984
  4.4 0.0 copy-start.3
  4.4 0.9 %copy-done.3 = f32[384,128]{1,0:T(8,128)S(1)} copy-done((f32[384,128]{1,0:T(8,128)S(1)}, f32[384,128]{1,0:T(8,128)}, u32[]{:S(2)}) %copy-start.3) | copy-done | bytes 196632
  5.3 11.2 %shard_map.46 = bf16[8,32,401]{2,1,0:T(8,128)(2,1)S(1)} custom-call(f32[8,6030]{1,0:T(8,128)S(1)} %copy-done.2, f32[384,128]{1,0:T(8,128)S(1)} %copy-done.3, bf16[2,1536,768]{2,1,0:T(8,128)(2,1)S(1)} %copy-done, bf16[768,401]{1,0:T(8,128)(2,1)S(1)} %copy-done.1), custom_call_target="tpu_custom_call" | custom-call | tf_op jit(solution)/shard_map/pallas_call | solution.py:176
  16.5 0.7 %copy.6 = bf16[8,32,401]{2,1,0:T(8,128)(2,1)} copy(bf16[8,32,401]{2,1,0:T(8,128)(2,1)S(1)} %shard_map.46) | data formatting | bytes 410624
Async XLA Ops:
  0.0 2.3 %copy-start = (bf16[2,1536,768]{2,1,0:T(8,128)(2,1)S(1)}, bf16[2,1536,768]{2,1,0:T(8,128)(2,1)}, u32[]{:S(2)}) copy-start(bf16[2,1536,768]{2,1,0:T(8,128)(2,1)} %constant.7.clone.fwd_ref) | copy-start | bytes 14155780
  2.3 1.1 %copy-start.1 = (bf16[768,401]{1,0:T(8,128)(2,1)S(1)}, bf16[768,401]{1,0:T(8,128)(2,1)}, u32[]{:S(2)}) copy-start(bf16[768,401]{1,0:T(8,128)(2,1)} %constant.8.clone.inv_ref) | copy-start | bytes 1847812
  3.5 0.9 %copy-start.2 = (f32[8,6030]{1,0:T(8,128)S(1)}, f32[8,6030]{1,0:T(8,128)}, u32[]{:S(2)}) copy-start(f32[8,6030]{1,0:T(8,128)} %raw_ref.1) | copy-start | bytes 578884
  4.4 0.9 %copy-start.3 = (f32[384,128]{1,0:T(8,128)S(1)}, f32[384,128]{1,0:T(8,128)}, u32[]{:S(2)}) copy-start(f32[384,128]{1,0:T(8,128)} %constant.6.clone.filt_ref) | copy-start | bytes 589828
where the time goes:
time: 17.5 us; the launch traced here: 17.2 us
  Pallas kernels  11.2 us (64%)
  local copies, waits for them, and re-layouts  6.03 us (34%)
    pallas_call x1, Pallas kernels, on_device(): pl.pallas_call(functools.partial(kernel, groups, members), out_shape=jax....  11.2 us
    unnamed x9, local copies, waits for them, and re-layouts  6.03 us

commit v1 on v0

--- a/solution.py
+++ b/solution.py
@@ -18,7 +18,13 @@
 BLOCKS = -(-WLEN // LANES)
 REACH = 3 * LANES
 SPAN = 2 * LANES * (BLOCKS - 1) + REACH
+VMEM_LIMIT = 48 * 1024 * 1024
 MESH = pl.DeviceIdType.MESH
+
+
+def halves(table):
+    high = table.astype(jnp.bfloat16)
+    return np.stack([high, (table - high.astype(np.float64)).astype(jnp.bfloat16)])
 
 
 def filter_table():
@@ -28,16 +34,13 @@
     table = np.zeros((REACH, LANES))
     for n in range(LANES):
         table[2 * n : 2 * n + TAPS, n] = taps
-    return table.astype(np.float32)
-
-
-def forward_table():
-    phase = np.arange(WLEN)[:, None] * np.arange(1, NFREQ + 1)[None, :] % WLEN
+    return halves(table)
+
+
+def wave_table(times):
+    phase = times[:, None] * np.arange(1, NFREQ + 1)[None, :] % WLEN
     angle = 2.0 * np.pi * phase / WLEN
-    table = np.zeros((BLOCKS * LANES, 2 * NFREQ))
-    table[:WLEN] = np.concatenate([np.cos(angle), -np.sin(angle)], axis=1)
-    high = table.astype(jnp.bfloat16)
-    return np.stack([high, (table - high.astype(np.float64)).astype(jnp.bfloat16)])
+    return np.concatenate([np.cos(angle), -np.sin(angle)], axis=1)
 
 
 def inverse_table():
@@ -47,14 +50,26 @@
     return np.concatenate([np.cos(angle), -np.sin(angle)], axis=0).astype(jnp.bfloat16)
 
 
-def kernel(groups, members, raw_ref, filt_ref, fwd_ref, inv_ref, out_ref,
-           padded, blocks, gathered, cross, send_sem, recv_sem):
+def split_dot(left, right):
+    high = left.astype(jnp.bfloat16)
+    low = (left - high.astype(jnp.float32)).astype(jnp.bfloat16)
+    return jnp.dot(jnp.concatenate([high, low, high], axis=1),
+                   jnp.concatenate([right[0], right[0], right[1]], axis=0),
+                   preferred_element_type=jnp.float32)
+
+
+def kernel(groups, members, *refs):
+    operands, out_ref = refs[:5], refs[5]
+    held, (padded, blocks, gathered, cross, load_sem, send_sem, recv_sem) = refs[6:11], refs[11:]
+    raw_ref, filt_ref, near_ref, far_ref, inv_ref = held
     count = groups * members
     grp, mem = lax.axis_index("grp"), lax.axis_index("mem")
     me = grp * members + mem
     channels, length = raw_ref.shape
-    lags = inv_ref.shape[1]
-
+
+    loads = [pltpu.make_async_copy(operands[i], held[i], load_sem.at[i]) for i in range(5)]
+    for load in loads:
+        load.start()
     barrier = pltpu.get_barrier_semaphore()
 
     def greet(step, carry):
@@ -67,6 +82,7 @@
 
     whole = length // LANES * LANES
     padded[:, whole:] = jnp.zeros((channels, padded.shape[1] - whole), jnp.float32)
+    loads[0].wait()
     padded[:, :length] = raw_ref[...]
     for w in range(WINDOWS):
         start = 2 * WLEN * w
@@ -79,29 +95,37 @@
         for b in range(BLOCKS):
             row = (w * BLOCKS + b) * channels
             blocks[row : row + channels, :] = piece[:, 2 * LANES * b : 2 * LANES * b + REACH]
-    decimated = jnp.dot(blocks[...], filt_ref[...], precision=lax.Precision.HIGHEST,
-                        preferred_element_type=jnp.float32)
-    frames = jnp.concatenate(
-        [
-            jnp.concatenate(
-                [
-                    decimated[(w * BLOCKS + b) * channels : (w * BLOCKS + b + 1) * channels, :]
-                    for b in range(BLOCKS)
-                ],
-                axis=1,
-            )
-            for w in range(WINDOWS)
-        ],
-        axis=0,
-    )
-    rows = WINDOWS * channels
-    high = frames.astype(jnp.bfloat16)
-    low = (frames - high.astype(jnp.float32)).astype(jnp.bfloat16)
-    parts = jnp.dot(jnp.concatenate([high, low], axis=0), fwd_ref[0],
-                    preferred_element_type=jnp.float32)
-    spec = parts[:rows] + parts[rows:]
-    spec = spec + jnp.dot(high, fwd_ref[1], preferred_element_type=jnp.float32)
-    spec_re, spec_im = spec[:, :NFREQ], spec[:, NFREQ:]
+    loads[1].wait()
+    decimated = split_dot(blocks[...], filt_ref)
+    inside = lax.broadcasted_iota(jnp.int32, (channels, LANES), 1) < WLEN - (BLOCKS - 1) * LANES
+    kept = []
+    for w in range(WINDOWS):
+        first = w * BLOCKS * channels
+        last = first + (BLOCKS - 1) * channels
+        kept += [decimated[first:last], jnp.where(inside, decimated[last : last + channels], 0.0)]
+    decimated = jnp.concatenate(kept, axis=0)
+
+    loads[2].wait()
+    parts = split_dot(decimated, near_ref)
+    loads[3].wait()
+    sums_re, sums_im = [], []
+    for w in range(WINDOWS):
+        sum_re = sum_im = None
+        for b in range(BLOCKS):
+            row = (w * BLOCKS + b) * channels
+            part_re = parts[row : row + channels, :NFREQ]
+            part_im = parts[row : row + channels, NFREQ:]
+            turn_re = far_ref[b : b + 1, :NFREQ]
+            turn_im = far_ref[b : b + 1, NFREQ:]
+            if b == 0:
+                sum_re, sum_im = part_re, part_im
+            else:
+                sum_re = sum_re + (part_re * turn_re - part_im * turn_im)
+                sum_im = sum_im + (part_re * turn_im + part_im * turn_re)
+        sums_re.append(sum_re)
+        sums_im.append(sum_im)
+    spec_re = jnp.concatenate(sums_re, axis=0)
+    spec_im = jnp.concatenate(sums_im, axis=0)
     power = spec_re * spec_re + spec_im * spec_im
     level = 0.01 * jnp.mean(power, axis=1, keepdims=True)
     factor = 1.0 / jnp.sqrt(power + level + 1e-06)
@@ -135,6 +159,8 @@
     at = lax.broadcasted_iota(jnp.int32, (size, size), 1)
     order = (lax.rem(to, panel) * channels + to // panel == at).astype(jnp.float32).astype(jnp.bfloat16)
     scale = 1.0 / math.sqrt(WINDOWS * NFREQ)
+
+    loads[4].wait()
 
     def work(index, carry):
         for j in range(panel):
@@ -168,28 +194,36 @@
 def solution(mesh):
     groups, members = mesh.shape["grp"], mesh.shape["mem"]
     count = groups * members
-    filt, fwd, inv = filter_table(), forward_table(), inverse_table()
+    tables = [
+        filter_table(),
+        halves(wave_table(np.arange(LANES))),
+        wave_table(LANES * np.arange(BLOCKS)).astype(np.float32),
+        inverse_table(),
+    ]
 
     def on_device(raw_traces):
         channels, length = raw_traces.shape
         start = 2 * WLEN * (WINDOWS - 1) // LANES * LANES
+        operands = [raw_traces] + [jnp.asarray(table) for table in tables]
         return pl.pallas_call(
             functools.partial(kernel, groups, members),
-            out_shape=jax.ShapeDtypeStruct((channels, count, inv.shape[1]), jnp.bfloat16),
-            in_specs=[pl.BlockSpec(memory_space=pltpu.VMEM)] * 4,
+            out_shape=jax.ShapeDtypeStruct((channels, count, 2 * MAXLAG + 1), jnp.bfloat16),
+            in_specs=[pl.BlockSpec(memory_space=pltpu.HBM)] * len(operands),
             out_specs=pl.BlockSpec(memory_space=pltpu.VMEM),
-            scratch_shapes=[
+            scratch_shapes=[pltpu.VMEM(x.shape, x.dtype) for x in operands]
+            + [
                 pltpu.VMEM((channels, start + SPAN + LANES), jnp.float32),
                 pltpu.VMEM((WINDOWS * BLOCKS * channels, REACH), jnp.float32),
                 pltpu.VMEM((count, WINDOWS, 2 * NFREQ), jnp.bfloat16),
                 pltpu.VMEM((min(count, 32) * channels, 2 * NFREQ), jnp.float32),
+                pltpu.SemaphoreType.DMA((len(operands),)),
                 pltpu.SemaphoreType.DMA,
                 pltpu.SemaphoreType.DMA,
             ],
             compiler_params=pltpu.CompilerParams(
-                collective_id=0, has_side_effects=True, vmem_limit_bytes=48 * 1024 * 1024
+                collective_id=0, has_side_effects=True, vmem_limit_bytes=VMEM_LIMIT
             ),
-        )(raw_traces, jnp.asarray(filt), jnp.asarray(fwd), jnp.asarray(inv))
+        )(*operands)
 
     return jax.shard_map(
         on_device,

time: 17.5 us -> 17.4 us (level)
  local copies, waits for them, and re-layouts: 6.03 us -> 5.48 us
  Pallas kernels: 11.2 us -> 11.6 us
    unnamed x9 -> x11, local copies, waits for them, and re-layouts: 6.03 us -> 5.48 us
    pallas_call x1, Pallas kernels: 11.2 us -> 11.6 us  [on_device(): pl.pallas_call(functools.partial(kernel, groups, members), out_shape=jax....]
where the time goes in v1:
time: 17.4 us; the launch traced here: 17.1 us
  Pallas kernels  11.6 us (67%)
  local copies, waits for them, and re-layouts  5.48 us (31%)
    pallas_call x1, Pallas kernels, on_device(): pl.pallas_call(functools.partial(kernel, groups, members), out_shape=jax....  11.6 us
    unnamed x11, local copies, waits for them, and re-layouts  5.48 us

profile of v1, /device:TPU:0, one launch (start us, length us, event | category | flops | bytes accessed | tf_op | source)
XLA Modules:
  0.0 17.1 jit_solution(8242471086929239082)
XLA Ops:
  0.0 0.0 copy-start
  0.0 1.1 %copy-done = bf16[768,401]{1,0:T(8,128)(2,1)S(1)} copy-done((bf16[768,401]{1,0:T(8,128)(2,1)S(1)}, bf16[768,401]{1,0:T(8,128)(2,1)}, u32[]{:S(2)}) %copy-start) | copy-done | bytes 615960
  1.1 0.0 copy-start.1
  1.1 1.0 %copy-done.1 = bf16[2,128,768]{2,1,0:T(8,128)(2,1)S(1)} copy-done((bf16[2,128,768]{2,1,0:T(8,128)(2,1)S(1)}, bf16[2,128,768]{2,1,0:T(8,128)(2,1)}, u32[]{:S(2)}) %copy-start.1) | copy-done | bytes 393240
  2.1 0.0 copy-start.2
  2.1 0.9 %copy-done.2 = f32[8,6030]{1,0:T(8,128)S(1)} copy-done((f32[8,6030]{1,0:T(8,128)S(1)}, f32[8,6030]{1,0:T(8,128)}, u32[]{:S(2)}) %copy-start.2) | copy-done | bytes 192984
  3.1 0.0 copy-start.3
  3.1 0.9 %copy-done.3 = bf16[2,384,128]{2,1,0:T(8,128)(2,1)S(1)} copy-done((bf16[2,384,128]{2,1,0:T(8,128)(2,1)S(1)}, bf16[2,384,128]{2,1,0:T(8,128)(2,1)}, u32[]{:S(2)}) %copy-start.3) | copy-done | bytes 196632
  4.0 0.0 copy-start.4
  4.0 0.8 %copy-done.4 = f32[12,768]{1,0:T(8,128)S(1)} copy-done((f32[12,768]{1,0:T(8,128)S(1)}, f32[12,768]{1,0:T(8,128)}, u32[]{:S(2)}) %copy-start.4) | copy-done | bytes 36888
  4.8 11.6 %shard_map.55 = bf16[8,32,401]{2,1,0:T(8,128)(2,1)S(1)} custom-call(f32[8,6030]{1,0:T(8,128)S(1)} %copy-done.2, bf16[2,384,128]{2,1,0:T(8,128)(2,1)S(1)} %copy-done.3, bf16[2,128,768]{2,1,0:T(8,128)(2,1)S(1)} %copy-done.1, f32[12,768]{1,0:T(8,128)S(1)} %copy-done.4, bf16[768,401]{1,0:T(8,128)(2,1)S(1)} %copy-done), custom_call_target="tpu_custom_call" | custom-call | tf_op jit(solution)/shard_map/pallas_call | solution.py:208
  16.4 0.7 %copy.7 = bf16[8,32,401]{2,1,0:T(8,128)(2,1)} copy(bf16[8,32,401]{2,1,0:T(8,128)(2,1)S(1)} %shard_map.55) | data formatting | bytes 410624
Async XLA Ops:
  0.0 1.1 %copy-start = (bf16[768,401]{1,0:T(8,128)(2,1)S(1)}, bf16[768,401]{1,0:T(8,128)(2,1)}, u32[]{:S(2)}) copy-start(bf16[768,401]{1,0:T(8,128)(2,1)} %constant.11.clone.refs_4_) | copy-start | bytes 1847812
  1.1 1.0 %copy-start.1 = (bf16[2,128,768]{2,1,0:T(8,128)(2,1)S(1)}, bf16[2,128,768]{2,1,0:T(8,128)(2,1)}, u32[]{:S(2)}) copy-start(bf16[2,128,768]{2,1,0:T(8,128)(2,1)} %constant.9.clone.refs_2_) | copy-start | bytes 1179652
  2.1 0.9 %copy-start.2 = (f32[8,6030]{1,0:T(8,128)S(1)}, f32[8,6030]{1,0:T(8,128)}, u32[]{:S(2)}) copy-start(f32[8,6030]{1,0:T(8,128)} %refs_0_.1) | copy-start | bytes 578884
  3.1 0.9 %copy-start.3 = (bf16[2,384,128]{2,1,0:T(8,128)(2,1)S(1)}, bf16[2,384,128]{2,1,0:T(8,128)(2,1)}, u32[]{:S(2)}) copy-start(bf16[2,384,128]{2,1,0:T(8,128)(2,1)} %constant.8.clone.refs_1_) | copy-start | bytes 589828
  4.0 0.8 %copy-start.4 = (f32[12,768]{1,0:T(8,128)S(1)}, f32[12,768]{1,0:T(8,128)}, u32[]{:S(2)}) copy-start(f32[12,768]{1,0:T(8,128)} %constant.10.clone.refs_3_) | copy-start | bytes 110596

commit v2 on v1

--- a/solution.py
+++ b/solution.py
@@ -19,7 +19,7 @@
 REACH = 3 * LANES
 SPAN = 2 * LANES * (BLOCKS - 1) + REACH
 VMEM_LIMIT = 48 * 1024 * 1024
-MESH = pl.DeviceIdType.MESH
+LOGICAL = pl.DeviceIdType.LOGICAL
 
 
 def halves(table):
@@ -58,9 +58,16 @@
                    preferred_element_type=jnp.float32)
 
 
+def whiten(spec_re, spec_im):
+    power = spec_re * spec_re + spec_im * spec_im
+    level = 0.01 * jnp.mean(power, axis=1, keepdims=True)
+    factor = 1.0 / jnp.sqrt(power + level + 1e-06)
+    return jnp.concatenate([spec_re * factor, spec_im * factor], axis=1).astype(jnp.bfloat16)
+
+
 def kernel(groups, members, *refs):
     operands, out_ref = refs[:5], refs[5]
-    held, (padded, blocks, gathered, cross, load_sem, send_sem, recv_sem) = refs[6:11], refs[11:]
+    held, (padded, lead, blocks, gathered, cross, load_sem, send_sem, recv_sem) = refs[6:11], refs[11:]
     raw_ref, filt_ref, near_ref, far_ref, inv_ref = held
     count = groups * members
     grp, mem = lax.axis_index("grp"), lax.axis_index("mem")
@@ -72,10 +79,12 @@
         load.start()
     barrier = pltpu.get_barrier_semaphore()
 
+    def peer_of(step):
+        peer = me + step
+        return jnp.where(peer >= count, peer - count, peer)
+
     def greet(step, carry):
-        peer = lax.rem(me + step, count)
-        pl.semaphore_signal(barrier, inc=1, device_id=(peer // members, lax.rem(peer, members)),
-                            device_id_type=MESH)
+        pl.semaphore_signal(barrier, inc=1, device_id=peer_of(step), device_id_type=LOGICAL)
         return carry
 
     lax.fori_loop(1, count, greet, 0)
@@ -94,8 +103,47 @@
             piece = pltpu.roll(padded[:, base : base + width], width - (start - base), 1)
         for b in range(BLOCKS):
             row = (w * BLOCKS + b) * channels
-            blocks[row : row + channels, :] = piece[:, 2 * LANES * b : 2 * LANES * b + REACH]
+            block = piece[:, 2 * LANES * b : 2 * LANES * b + REACH]
+            blocks[row : row + channels, :] = block
+            lead[w * BLOCKS + b : w * BLOCKS + b + 1, :] = block[:1]
+
     loads[1].wait()
+    first = split_dot(lead[...], filt_ref)
+    row = lax.broadcasted_iota(jnp.int32, first.shape, 0)
+    beyond = lax.broadcasted_iota(jnp.int32, first.shape, 1) >= WLEN - (BLOCKS - 1) * LANES
+    first = jnp.where((lax.rem(row, BLOCKS) == BLOCKS - 1) & beyond, 0.0, first)
+    loads[2].wait()
+    parts = split_dot(first, near_ref)
+    loads[3].wait()
+    part_re, part_im = parts[:, :NFREQ], parts[:, NFREQ:]
+    turn_re, turn_im = far_ref[:, :NFREQ], far_ref[:, NFREQ:]
+    window = lax.broadcasted_iota(jnp.int32, part_re.shape, 0) // BLOCKS
+    sums = []
+    for turned in (part_re * turn_re - part_im * turn_im, part_re * turn_im + part_im * turn_re):
+        sums.append(jnp.concatenate(
+            [
+                jnp.sum(jnp.where(window == w, turned, 0.0), axis=0, keepdims=True)
+                for w in range(WINDOWS)
+            ],
+            axis=0,
+        ))
+    gathered[me] = whiten(*sums)
+
+    pl.semaphore_wait(barrier, count - 1)
+
+    def send(step, carry):
+        pltpu.make_async_remote_copy(
+            src_ref=gathered.at[me],
+            dst_ref=gathered.at[me],
+            send_sem=send_sem,
+            recv_sem=recv_sem,
+            device_id=peer_of(step),
+            device_id_type=LOGICAL,
+        ).start()
+        return carry
+
+    lax.fori_loop(1, count, send, 0)
+
     decimated = split_dot(blocks[...], filt_ref)
     inside = lax.broadcasted_iota(jnp.int32, (channels, LANES), 1) < WLEN - (BLOCKS - 1) * LANES
     kept = []
@@ -105,9 +153,7 @@
         kept += [decimated[first:last], jnp.where(inside, decimated[last : last + channels], 0.0)]
     decimated = jnp.concatenate(kept, axis=0)
 
-    loads[2].wait()
     parts = split_dot(decimated, near_ref)
-    loads[3].wait()
     sums_re, sums_im = [], []
     for w in range(WINDOWS):
         sum_re = sum_im = None
@@ -126,32 +172,9 @@
         sums_im.append(sum_im)
     spec_re = jnp.concatenate(sums_re, axis=0)
     spec_im = jnp.concatenate(sums_im, axis=0)
-    power = spec_re * spec_re + spec_im * spec_im
-    level = 0.01 * jnp.mean(power, axis=1, keepdims=True)
-    factor = 1.0 / jnp.sqrt(power + level + 1e-06)
-    white = jnp.concatenate([spec_re * factor, spec_im * factor], axis=1)
-    own = white.astype(jnp.bfloat16).astype(jnp.float32)
-    gathered[me] = jnp.concatenate(
-        [own[w * channels : w * channels + 1] for w in range(WINDOWS)], axis=0
-    ).astype(jnp.bfloat16)
-
-    pl.semaphore_wait(barrier, count - 1)
-
-    def send(step, carry):
-        peer = lax.rem(me + step, count)
-        pltpu.make_async_remote_copy(
-            src_ref=gathered.at[me],
-            dst_ref=gathered.at[me],
-            send_sem=send_sem,
-            recv_sem=recv_sem,
-            device_id=(peer // members, lax.rem(peer, members)),
-            device_id_type=MESH,
-        ).start()
-        return carry
-
-    lax.fori_loop(1, count, send, 0)
+    own = whiten(spec_re, spec_im).astype(jnp.float32)
+
     others = gathered.at[pl.ds(0, count - 1)]
-    pltpu.make_async_copy(others, others, recv_sem).wait()
 
     panel = min(count, 32)
     size = panel * channels
@@ -161,6 +184,7 @@
     scale = 1.0 / math.sqrt(WINDOWS * NFREQ)
 
     loads[4].wait()
+    pltpu.make_async_copy(others, others, recv_sem).wait()
 
     def work(index, carry):
         for j in range(panel):
@@ -197,22 +221,26 @@
     tables = [
         filter_table(),
         halves(wave_table(np.arange(LANES))),
-        wave_table(LANES * np.arange(BLOCKS)).astype(np.float32),
+        np.tile(wave_table(LANES * np.arange(BLOCKS)), (WINDOWS, 1)).astype(np.float32),
         inverse_table(),
     ]
 
     def on_device(raw_traces):
         channels, length = raw_traces.shape
         start = 2 * WLEN * (WINDOWS - 1) // LANES * LANES
-        operands = [raw_traces] + [jnp.asarray(table) for table in tables]
+        operands = [
+            pltpu.with_memory_space_constraint(x, pltpu.HBM)
+            for x in [raw_traces] + [jnp.asarray(table) for table in tables]
+        ]
         return pl.pallas_call(
             functools.partial(kernel, groups, members),
             out_shape=jax.ShapeDtypeStruct((channels, count, 2 * MAXLAG + 1), jnp.bfloat16),
-            in_specs=[pl.BlockSpec(memory_space=pltpu.HBM)] * len(operands),
+            in_specs=[pl.BlockSpec(memory_space=pl.ANY)] * len(operands),
             out_specs=pl.BlockSpec(memory_space=pltpu.VMEM),
             scratch_shapes=[pltpu.VMEM(x.shape, x.dtype) for x in operands]
             + [
                 pltpu.VMEM((channels, start + SPAN + LANES), jnp.float32),
+                pltpu.VMEM((WINDOWS * BLOCKS, REACH), jnp.float32),
                 pltpu.VMEM((WINDOWS * BLOCKS * channels, REACH), jnp.float32),
                 pltpu.VMEM((count, WINDOWS, 2 * NFREQ), jnp.bfloat16),
                 pltpu.VMEM((min(count, 32) * channels, 2 * NFREQ), jnp.float32),

time: 17.4 us -> 11.7 us (0.67)
  local copies, waits for them, and re-layouts: 5.48 us -> 0.71 us
  Pallas kernels: 11.6 us -> 10.9 us
    unnamed x11 -> x1, local copies, waits for them, and re-layouts: 5.48 us -> 0.71 us
    pallas_call x1, Pallas kernels: 11.6 us -> 10.9 us  [on_device(): pl.pallas_call(functools.partial(kernel, groups, members), out_shape=jax....]
where the time goes in v2:
time: 11.7 us; the launch traced here: 11.6 us
  Pallas kernels  10.9 us (93%)
  local copies, waits for them, and re-layouts  0.71 us (6%)
    pallas_call x1, Pallas kernels, on_device(): pl.pallas_call(functools.partial(kernel, groups, members), out_shape=jax....  10.9 us
    unnamed x1, local copies, waits for them, and re-layouts  0.71 us

profile of v2, /device:TPU:0, one launch (start us, length us, event | category | flops | bytes accessed | tf_op | source)
XLA Modules:
  0.0 11.6 jit_solution(2177853493228407004)
XLA Ops:
  0.0 10.9 %shard_map.55 = bf16[8,32,401]{2,1,0:T(8,128)(2,1)S(1)} custom-call(f32[8,6030]{1,0:T(8,128)} %refs_0_.1, bf16[2,384,128]{2,1,0:T(8,128)(2,1)} %constant.8.clone.refs_1_, bf16[2,128,768]{2,1,0:T(8,128)(2,1)} %constant.9.clone.refs_2_, f32[24,768]{1,0:T(8,128)} %constant.10.clone.refs_3_, bf16[768,401]{1,0:T(8,128)(2,1)} %constant.11.clone.refs_4_), custom_call_target="tpu_custom_call" | custom-call | tf_op jit(solution)/shard_map/pallas_call | solution.py:235
  10.9 0.7 %copy.7 = bf16[8,32,401]{2,1,0:T(8,128)(2,1)} copy(bf16[8,32,401]{2,1,0:T(8,128)(2,1)S(1)} %shard_map.55) | data formatting | bytes 410624

commit v3 on v2

--- a/solution.py
+++ b/solution.py
@@ -18,6 +18,8 @@
 BLOCKS = -(-WLEN // LANES)
 REACH = 3 * LANES
 SPAN = 2 * LANES * (BLOCKS - 1) + REACH
+PIECES = 2 * NFREQ // LANES
+SLOT = 16
 VMEM_LIMIT = 48 * 1024 * 1024
 LOGICAL = pl.DeviceIdType.LOGICAL
 
@@ -62,12 +64,12 @@
     power = spec_re * spec_re + spec_im * spec_im
     level = 0.01 * jnp.mean(power, axis=1, keepdims=True)
     factor = 1.0 / jnp.sqrt(power + level + 1e-06)
-    return jnp.concatenate([spec_re * factor, spec_im * factor], axis=1).astype(jnp.bfloat16)
+    return jnp.concatenate([spec_re * factor, spec_im * factor], axis=1)
 
 
 def kernel(groups, members, *refs):
     operands, out_ref = refs[:5], refs[5]
-    held, (padded, lead, blocks, gathered, cross, load_sem, send_sem, recv_sem) = refs[6:11], refs[11:]
+    held, (padded, lead, blocks, gathered, wide, cross, load_sem, send_sem, recv_sem) = refs[6:11], refs[11:]
     raw_ref, filt_ref, near_ref, far_ref, inv_ref = held
     count = groups * members
     grp, mem = lax.axis_index("grp"), lax.axis_index("mem")
@@ -80,19 +82,20 @@
     barrier = pltpu.get_barrier_semaphore()
 
     def peer_of(step):
-        peer = me + step
+        peer = me + jnp.where(step < count // 2, step + count // 2, step - count // 2 + 1)
         return jnp.where(peer >= count, peer - count, peer)
 
     def greet(step, carry):
         pl.semaphore_signal(barrier, inc=1, device_id=peer_of(step), device_id_type=LOGICAL)
         return carry
 
-    lax.fori_loop(1, count, greet, 0)
+    lax.fori_loop(0, count - 1, greet, 0)
 
     whole = length // LANES * LANES
     padded[:, whole:] = jnp.zeros((channels, padded.shape[1] - whole), jnp.float32)
     loads[0].wait()
     padded[:, :length] = raw_ref[...]
+    pieces = []
     for w in range(WINDOWS):
         start = 2 * WLEN * w
         base = start // LANES * LANES
@@ -101,11 +104,10 @@
         else:
             width = SPAN + LANES
             piece = pltpu.roll(padded[:, base : base + width], width - (start - base), 1)
+        pieces.append(piece)
         for b in range(BLOCKS):
-            row = (w * BLOCKS + b) * channels
-            block = piece[:, 2 * LANES * b : 2 * LANES * b + REACH]
-            blocks[row : row + channels, :] = block
-            lead[w * BLOCKS + b : w * BLOCKS + b + 1, :] = block[:1]
+            row = w * BLOCKS + b
+            lead[row : row + 1, :] = piece[:1, 2 * LANES * b : 2 * LANES * b + REACH]
 
     loads[1].wait()
     first = split_dot(lead[...], filt_ref)
@@ -127,7 +129,15 @@
             ],
             axis=0,
         ))
-    gathered[me] = whiten(*sums)
+    white = whiten(*sums)
+    gathered[me] = jnp.concatenate(
+        [
+            white[w : w + 1, LANES * i : LANES * (i + 1)]
+            for w in range(WINDOWS)
+            for i in range(PIECES)
+        ],
+        axis=0,
+    ).astype(jnp.bfloat16)
 
     pl.semaphore_wait(barrier, count - 1)
 
@@ -142,8 +152,12 @@
         ).start()
         return carry
 
-    lax.fori_loop(1, count, send, 0)
-
+    lax.fori_loop(0, count - 1, send, 0)
+
+    for w in range(WINDOWS):
+        for b in range(BLOCKS):
+            row = (w * BLOCKS + b) * channels
+            blocks[row : row + channels, :] = pieces[w][:, 2 * LANES * b : 2 * LANES * b + REACH]
     decimated = split_dot(blocks[...], filt_ref)
     inside = lax.broadcasted_iota(jnp.int32, (channels, LANES), 1) < WLEN - (BLOCKS - 1) * LANES
     kept = []
@@ -172,15 +186,11 @@
         sums_im.append(sum_im)
     spec_re = jnp.concatenate(sums_re, axis=0)
     spec_im = jnp.concatenate(sums_im, axis=0)
-    own = whiten(spec_re, spec_im).astype(jnp.float32)
+    own = whiten(spec_re, spec_im).astype(jnp.bfloat16).astype(jnp.float32)
 
     others = gathered.at[pl.ds(0, count - 1)]
 
     panel = min(count, 32)
-    size = panel * channels
-    to = lax.broadcasted_iota(jnp.int32, (size, size), 0)
-    at = lax.broadcasted_iota(jnp.int32, (size, size), 1)
-    order = (lax.rem(to, panel) * channels + to // panel == at).astype(jnp.float32).astype(jnp.bfloat16)
     scale = 1.0 / math.sqrt(WINDOWS * NFREQ)
 
     loads[4].wait()
@@ -188,21 +198,24 @@
 
     def work(index, carry):
         for j in range(panel):
-            source = gathered[index * panel + j].astype(jnp.float32)
-            cross_re = jnp.zeros((channels, NFREQ), jnp.float32)
-            cross_im = jnp.zeros((channels, NFREQ), jnp.float32)
-            for w in range(WINDOWS):
-                a_re = own[w * channels : (w + 1) * channels, :NFREQ]
-                a_im = own[w * channels : (w + 1) * channels, NFREQ:]
-                b_re = source[w : w + 1, :NFREQ]
-                b_im = source[w : w + 1, NFREQ:]
-                cross_re = cross_re + (a_re * b_re + a_im * b_im)
-                cross_im = cross_im + (a_im * b_re - a_re * b_im)
-            cross[j * channels : (j + 1) * channels, :NFREQ] = cross_re
-            cross[j * channels : (j + 1) * channels, NFREQ:] = cross_im
-        turned = jnp.dot(order, cross[...].astype(jnp.bfloat16),
-                         preferred_element_type=jnp.float32).astype(jnp.bfloat16)
-        corr = jnp.dot(turned, inv_ref[...], preferred_element_type=jnp.float32) * scale
+            wide[j * SLOT : j * SLOT + WINDOWS * PIECES, :] = gathered[index * panel + j].astype(jnp.float32)
+        half = PIECES // 2
+        for i in range(half):
+            real, imag = slice(LANES * i, LANES * (i + 1)), slice(NFREQ + LANES * i, NFREQ + LANES * (i + 1))
+            b_re = [wide[pl.ds(w * PIECES + i, panel, stride=SLOT), :] for w in range(WINDOWS)]
+            b_im = [wide[pl.ds(w * PIECES + half + i, panel, stride=SLOT), :] for w in range(WINDOWS)]
+            for c in range(channels):
+                cross_re = cross_im = None
+                for w in range(WINDOWS):
+                    a_re = own[w * channels + c : w * channels + c + 1, real]
+                    a_im = own[w * channels + c : w * channels + c + 1, imag]
+                    term_re = a_re * b_re[w] + a_im * b_im[w]
+                    term_im = a_im * b_re[w] - a_re * b_im[w]
+                    cross_re = term_re if w == 0 else cross_re + term_re
+                    cross_im = term_im if w == 0 else cross_im + term_im
+                cross[c * panel : (c + 1) * panel, real] = cross_re.astype(jnp.bfloat16)
+                cross[c * panel : (c + 1) * panel, imag] = cross_im.astype(jnp.bfloat16)
+        corr = jnp.dot(cross[...], inv_ref[...], preferred_element_type=jnp.float32) * scale
         corr = corr.astype(jnp.bfloat16)
         for c in range(channels):
             out_ref[c, pl.ds(pl.multiple_of(index * panel, panel), panel), :] = corr[c * panel : (c + 1) * panel]
@@ -242,8 +255,9 @@
                 pltpu.VMEM((channels, start + SPAN + LANES), jnp.float32),
                 pltpu.VMEM((WINDOWS * BLOCKS, REACH), jnp.float32),
                 pltpu.VMEM((WINDOWS * BLOCKS * channels, REACH), jnp.float32),
-                pltpu.VMEM((count, WINDOWS, 2 * NFREQ), jnp.bfloat16),
-                pltpu.VMEM((min(count, 32) * channels, 2 * NFREQ), jnp.float32),
+                pltpu.VMEM((count, WINDOWS * PIECES, LANES), jnp.bfloat16),
+                pltpu.VMEM((min(count, 32) * SLOT, LANES), jnp.float32),
+                pltpu.VMEM((min(count, 32) * channels, 2 * NFREQ), jnp.bfloat16),
                 pltpu.SemaphoreType.DMA((len(operands),)),
                 pltpu.SemaphoreType.DMA,
                 pltpu.SemaphoreType.DMA,

time: 11.7 us -> 12.7 us (1.085)
  Pallas kernels: 10.9 us -> 11.8 us
    pallas_call x1, Pallas kernels: 10.9 us -> 11.8 us  [on_device(): pl.pallas_call(functools.partial(kernel, groups, members), out_shape=jax....]
where the time goes in v3:
time: 12.7 us; the launch traced here: 12.5 us
  Pallas kernels  11.8 us (93%)
  local copies, waits for them, and re-layouts  0.71 us (6%)
    pallas_call x1, Pallas kernels, on_device(): pl.pallas_call(functools.partial(kernel, groups, members), out_shape=jax....  11.8 us
    unnamed x1, local copies, waits for them, and re-layouts  0.71 us

profile of v3, /device:TPU:0, one launch (start us, length us, event | category | flops | bytes accessed | tf_op | source)
XLA Modules:
  0.0 12.5 jit_solution(675185143320274599)
XLA Ops:
  0.0 11.8 %shard_map.55 = bf16[8,32,401]{2,1,0:T(8,128)(2,1)S(1)} custom-call(f32[8,6030]{1,0:T(8,128)} %refs_0_.1, bf16[2,384,128]{2,1,0:T(8,128)(2,1)} %constant.8.clone.refs_1_, bf16[2,128,768]{2,1,0:T(8,128)(2,1)} %constant.9.clone.refs_2_, f32[24,768]{1,0:T(8,128)} %constant.10.clone.refs_3_, bf16[768,401]{1,0:T(8,128)(2,1)} %constant.11.clone.refs_4_), custom_call_target="tpu_custom_call" | custom-call | tf_op jit(solution)/shard_map/pallas_call | solution.py:248
  11.8 0.7 %copy.7 = bf16[8,32,401]{2,1,0:T(8,128)(2,1)} copy(bf16[8,32,401]{2,1,0:T(8,128)(2,1)S(1)} %shard_map.55) | data formatting | bytes 410624

commit v4 on v3

--- a/solution.py
+++ b/solution.py
@@ -82,14 +82,14 @@
     barrier = pltpu.get_barrier_semaphore()
 
     def peer_of(step):
-        peer = me + jnp.where(step < count // 2, step + count // 2, step - count // 2 + 1)
+        peer = me + step
         return jnp.where(peer >= count, peer - count, peer)
 
     def greet(step, carry):
         pl.semaphore_signal(barrier, inc=1, device_id=peer_of(step), device_id_type=LOGICAL)
         return carry
 
-    lax.fori_loop(0, count - 1, greet, 0)
+    lax.fori_loop(1, count, greet, 0)
 
     whole = length // LANES * LANES
     padded[:, whole:] = jnp.zeros((channels, padded.shape[1] - whole), jnp.float32)
@@ -152,7 +152,7 @@
         ).start()
         return carry
 
-    lax.fori_loop(0, count - 1, send, 0)
+    lax.fori_loop(1, count, send, 0)
 
     for w in range(WINDOWS):
         for b in range(BLOCKS):

time: 12.7 us -> 11.5 us (0.906)
  Pallas kernels: 11.8 us -> 10.7 us
    pallas_call x1, Pallas kernels: 11.8 us -> 10.7 us  [on_device(): pl.pallas_call(functools.partial(kernel, groups, members), out_shape=jax....]
where the time goes in v4:
time: 11.5 us; the launch traced here: 11.4 us
  Pallas kernels  10.7 us (93%)
  local copies, waits for them, and re-layouts  0.71 us (6%)
    pallas_call x1, Pallas kernels, on_device(): pl.pallas_call(functools.partial(kernel, groups, members), out_shape=jax....  10.7 us
    unnamed x1, local copies, waits for them, and re-layouts  0.71 us

profile of v4, /device:TPU:0, one launch (start us, length us, event | category | flops | bytes accessed | tf_op | source)
XLA Modules:
  0.0 11.4 jit_solution(11244524683365464117)
XLA Ops:
  0.0 10.7 %shard_map.55 = bf16[8,32,401]{2,1,0:T(8,128)(2,1)S(1)} custom-call(f32[8,6030]{1,0:T(8,128)} %refs_0_.1, bf16[2,384,128]{2,1,0:T(8,128)(2,1)} %constant.8.clone.refs_1_, bf16[2,128,768]{2,1,0:T(8,128)(2,1)} %constant.9.clone.refs_2_, f32[24,768]{1,0:T(8,128)} %constant.10.clone.refs_3_, bf16[768,401]{1,0:T(8,128)(2,1)} %constant.11.clone.refs_4_), custom_call_target="tpu_custom_call" | custom-call | tf_op jit(solution)/shard_map/pallas_call | solution.py:248
  10.7 0.7 %copy.7 = bf16[8,32,401]{2,1,0:T(8,128)(2,1)} copy(bf16[8,32,401]{2,1,0:T(8,128)(2,1)S(1)} %shard_map.55) | data formatting | bytes 410624

commit v5 on v4

--- a/solution.py
+++ b/solution.py
@@ -20,6 +20,7 @@
 SPAN = 2 * LANES * (BLOCKS - 1) + REACH
 PIECES = 2 * NFREQ // LANES
 SLOT = 16
+CHUNKS = 4
 VMEM_LIMIT = 48 * 1024 * 1024
 LOGICAL = pl.DeviceIdType.LOGICAL
 
@@ -69,11 +70,11 @@
 
 def kernel(groups, members, *refs):
     operands, out_ref = refs[:5], refs[5]
-    held, (padded, lead, blocks, gathered, wide, cross, load_sem, send_sem, recv_sem) = refs[6:11], refs[11:]
+    held, (padded, lead, blocks, gathered, wide, cross, load_sem, send_sem, recv_sem,
+           pass_send_sem, pass_recv_sem) = refs[6:11], refs[11:]
     raw_ref, filt_ref, near_ref, far_ref, inv_ref = held
     count = groups * members
     grp, mem = lax.axis_index("grp"), lax.axis_index("mem")
-    me = grp * members + mem
     channels, length = raw_ref.shape
 
     loads = [pltpu.make_async_copy(operands[i], held[i], load_sem.at[i]) for i in range(5)]
@@ -81,15 +82,22 @@
         load.start()
     barrier = pltpu.get_barrier_semaphore()
 
-    def peer_of(step):
-        peer = me + step
-        return jnp.where(peer >= count, peer - count, peer)
+    def wrap(position, size):
+        return jnp.where(position >= size, position - size, position)
+
+    def column_peer(step):
+        return wrap(grp + step, groups) * members + mem
+
+    def sibling(step):
+        return grp * members + wrap(mem + step, members)
 
     def greet(step, carry):
-        pl.semaphore_signal(barrier, inc=1, device_id=peer_of(step), device_id_type=LOGICAL)
+        pl.semaphore_signal(barrier, inc=1, device_id=column_peer(step), device_id_type=LOGICAL)
         return carry
 
-    lax.fori_loop(1, count, greet, 0)
+    lax.fori_loop(1, groups, greet, 0)
+    for step in range(1, members):
+        pl.semaphore_signal(barrier, inc=1, device_id=sibling(step), device_id_type=LOGICAL)
 
     whole = length // LANES * LANES
     padded[:, whole:] = jnp.zeros((channels, padded.shape[1] - whole), jnp.float32)
@@ -130,7 +138,7 @@
             axis=0,
         ))
     white = whiten(*sums)
-    gathered[me] = jnp.concatenate(
+    gathered[mem, grp] = jnp.concatenate(
         [
             white[w : w + 1, LANES * i : LANES * (i + 1)]
             for w in range(WINDOWS)
@@ -139,20 +147,22 @@
         axis=0,
     ).astype(jnp.bfloat16)
 
-    pl.semaphore_wait(barrier, count - 1)
+    pl.semaphore_wait(barrier, groups + members - 2)
+    chunk = groups // CHUNKS
+    mine = grp // chunk
 
     def send(step, carry):
         pltpu.make_async_remote_copy(
-            src_ref=gathered.at[me],
-            dst_ref=gathered.at[me],
+            src_ref=gathered.at[mem, grp],
+            dst_ref=gathered.at[mem, grp],
             send_sem=send_sem,
-            recv_sem=recv_sem,
-            device_id=peer_of(step),
+            recv_sem=recv_sem.at[mine],
+            device_id=column_peer(step),
             device_id_type=LOGICAL,
         ).start()
         return carry
 
-    lax.fori_loop(1, count, send, 0)
+    lax.fori_loop(1, groups, send, 0)
 
     for w in range(WINDOWS):
         for b in range(BLOCKS):
@@ -188,17 +198,36 @@
     spec_im = jnp.concatenate(sums_im, axis=0)
     own = whiten(spec_re, spec_im).astype(jnp.bfloat16).astype(jnp.float32)
 
-    others = gathered.at[pl.ds(0, count - 1)]
+    def await_bytes(ref, sem):
+        pltpu.make_async_copy(ref, ref, sem).wait()
+
+    await_bytes(gathered.at[0, pl.ds(0, chunk - 1)], recv_sem.at[mine])
+    for i in range(CHUNKS):
+        part = wrap(mine + i, CHUNKS)
+        if i > 0:
+            await_bytes(gathered.at[0, pl.ds(0, chunk)], recv_sem.at[part])
+        held_part = gathered.at[mem, pl.ds(part * chunk, chunk)]
+        for step in range(1, members):
+            pltpu.make_async_remote_copy(
+                src_ref=held_part,
+                dst_ref=held_part,
+                send_sem=pass_send_sem,
+                recv_sem=pass_recv_sem,
+                device_id=sibling(step),
+                device_id_type=LOGICAL,
+            ).start()
 
     panel = min(count, 32)
     scale = 1.0 / math.sqrt(WINDOWS * NFREQ)
 
     loads[4].wait()
-    pltpu.make_async_copy(others, others, recv_sem).wait()
+    await_bytes(gathered.at[pl.ds(0, members - 1)], pass_recv_sem)
 
     def work(index, carry):
         for j in range(panel):
-            wide[j * SLOT : j * SLOT + WINDOWS * PIECES, :] = gathered[index * panel + j].astype(jnp.float32)
+            wide[j * SLOT : j * SLOT + WINDOWS * PIECES, :] = gathered[
+                j % members, index * (panel // members) + j // members
+            ].astype(jnp.float32)
         half = PIECES // 2
         for i in range(half):
             real, imag = slice(LANES * i, LANES * (i + 1)), slice(NFREQ + LANES * i, NFREQ + LANES * (i + 1))
@@ -225,7 +254,8 @@
         work(0, 0)
     else:
         lax.fori_loop(0, count // panel, work, 0)
-    pltpu.make_async_copy(others, others, send_sem).wait()
+    await_bytes(gathered.at[0, pl.ds(0, groups - 1)], send_sem)
+    await_bytes(gathered.at[pl.ds(0, members - 1)], pass_send_sem)
 
 
 def solution(mesh):
@@ -255,10 +285,12 @@
                 pltpu.VMEM((channels, start + SPAN + LANES), jnp.float32),
                 pltpu.VMEM((WINDOWS * BLOCKS, REACH), jnp.float32),
                 pltpu.VMEM((WINDOWS * BLOCKS * channels, REACH), jnp.float32),
-                pltpu.VMEM((count, WINDOWS * PIECES, LANES), jnp.bfloat16),
+                pltpu.VMEM((members, groups, WINDOWS * PIECES, LANES), jnp.bfloat16),
                 pltpu.VMEM((min(count, 32) * SLOT, LANES), jnp.float32),
                 pltpu.VMEM((min(count, 32) * channels, 2 * NFREQ), jnp.bfloat16),
                 pltpu.SemaphoreType.DMA((len(operands),)),
+                pltpu.SemaphoreType.DMA,
+                pltpu.SemaphoreType.DMA((CHUNKS,)),
                 pltpu.SemaphoreType.DMA,
                 pltpu.SemaphoreType.DMA,
             ],

time: 11.5 us -> 12.3 us (1.070)
  the two profiles are of different devices: /device:TPU:0 before, /device:TPU:1 now
where the time goes in v5:
time: 12.3 us; the launch traced here: 12.2 us
  Pallas kernels  11.4 us (93%)
  local copies, waits for them, and re-layouts  0.71 us (6%)
    pallas_call x1, Pallas kernels, on_device(): pl.pallas_call(functools.partial(kernel, groups, members), out_shape=jax....  11.4 us
    unnamed x1, local copies, waits for them, and re-layouts  0.71 us

profile of v5, /device:TPU:1, one launch (start us, length us, event | category | flops | bytes accessed | tf_op | source)
XLA Modules:
  0.0 12.2 jit_solution(17116912629073850616)
XLA Ops:
  0.0 11.4 %shard_map.55 = bf16[8,32,401]{2,1,0:T(8,128)(2,1)S(1)} custom-call(f32[8,6030]{1,0:T(8,128)} %refs_0_.1, bf16[2,384,128]{2,1,0:T(8,128)(2,1)} %constant.8.clone.refs_1_, bf16[2,128,768]{2,1,0:T(8,128)(2,1)} %constant.9.clone.refs_2_, f32[24,768]{1,0:T(8,128)} %constant.10.clone.refs_3_, bf16[768,401]{1,0:T(8,128)(2,1)} %constant.11.clone.refs_4_), custom_call_target="tpu_custom_call" | custom-call | tf_op jit(solution)/shard_map/pallas_call | solution.py:278
  11.4 0.7 %copy.7 = bf16[8,32,401]{2,1,0:T(8,128)(2,1)} copy(bf16[8,32,401]{2,1,0:T(8,128)(2,1)S(1)} %shard_map.55) | data formatting | bytes 410624

commit v6 on v4

--- a/solution.py
+++ b/solution.py
@@ -20,6 +20,7 @@
 SPAN = 2 * LANES * (BLOCKS - 1) + REACH
 PIECES = 2 * NFREQ // LANES
 SLOT = 16
+HALVES = 2
 VMEM_LIMIT = 48 * 1024 * 1024
 LOGICAL = pl.DeviceIdType.LOGICAL
 
@@ -77,7 +78,7 @@
     channels, length = raw_ref.shape
 
     loads = [pltpu.make_async_copy(operands[i], held[i], load_sem.at[i]) for i in range(5)]
-    for load in loads:
+    for load in loads[:4]:
         load.start()
     barrier = pltpu.get_barrier_semaphore()
 
@@ -141,18 +142,23 @@
 
     pl.semaphore_wait(barrier, count - 1)
 
+    half = count // HALVES
+    mine = me // half
+
     def send(step, carry):
         pltpu.make_async_remote_copy(
             src_ref=gathered.at[me],
             dst_ref=gathered.at[me],
             send_sem=send_sem,
-            recv_sem=recv_sem,
+            recv_sem=recv_sem.at[mine],
             device_id=peer_of(step),
             device_id_type=LOGICAL,
         ).start()
         return carry
 
     lax.fori_loop(1, count, send, 0)
+
+    loads[4].start()
 
     for w in range(WINDOWS):
         for b in range(BLOCKS):
@@ -188,13 +194,8 @@
     spec_im = jnp.concatenate(sums_im, axis=0)
     own = whiten(spec_re, spec_im).astype(jnp.bfloat16).astype(jnp.float32)
 
-    others = gathered.at[pl.ds(0, count - 1)]
-
-    panel = min(count, 32)
+    panel = min(half, 32)
     scale = 1.0 / math.sqrt(WINDOWS * NFREQ)
-
-    loads[4].wait()
-    pltpu.make_async_copy(others, others, recv_sem).wait()
 
     def work(index, carry):
         for j in range(panel):
@@ -221,10 +222,18 @@
             out_ref[c, pl.ds(pl.multiple_of(index * panel, panel), panel), :] = corr[c * panel : (c + 1) * panel]
         return carry
 
-    if count == panel:
-        work(0, 0)
-    else:
-        lax.fori_loop(0, count // panel, work, 0)
+    loads[4].wait()
+    for i in range(HALVES):
+        part = mine + i
+        part = jnp.where(part >= HALVES, part - HALVES, part)
+        arrived = gathered.at[pl.ds(0, half - 1 if i == 0 else half)]
+        pltpu.make_async_copy(arrived, arrived, recv_sem.at[part]).wait()
+        if half == panel:
+            work(part, 0)
+        else:
+            panels = half // panel
+            lax.fori_loop(part * panels, (part + 1) * panels, work, 0)
+    others = gathered.at[pl.ds(0, count - 1)]
     pltpu.make_async_copy(others, others, send_sem).wait()
 
 
@@ -256,11 +265,11 @@
                 pltpu.VMEM((WINDOWS * BLOCKS, REACH), jnp.float32),
                 pltpu.VMEM((WINDOWS * BLOCKS * channels, REACH), jnp.float32),
                 pltpu.VMEM((count, WINDOWS * PIECES, LANES), jnp.bfloat16),
-                pltpu.VMEM((min(count, 32) * SLOT, LANES), jnp.float32),
-                pltpu.VMEM((min(count, 32) * channels, 2 * NFREQ), jnp.bfloat16),
+                pltpu.VMEM((min(count // HALVES, 32) * SLOT, LANES), jnp.float32),
+                pltpu.VMEM((min(count // HALVES, 32) * channels, 2 * NFREQ), jnp.bfloat16),
                 pltpu.SemaphoreType.DMA((len(operands),)),
                 pltpu.SemaphoreType.DMA,
-                pltpu.SemaphoreType.DMA,
+                pltpu.SemaphoreType.DMA((HALVES,)),
             ],
             compiler_params=pltpu.CompilerParams(
                 collective_id=0, has_side_effects=True, vmem_limit_bytes=VMEM_LIMIT

time: 11.5 us -> 11.4 us (level)
  Pallas kernels: 10.7 us -> 10.5 us
    pallas_call x1, Pallas kernels: 10.7 us -> 10.5 us  [on_device(): pl.pallas_call(functools.partial(kernel, groups, members), out_shape=jax....]
where the time goes in v6:
time: 11.4 us; the launch traced here: 11.3 us
  Pallas kernels  10.5 us (92%)
  local copies, waits for them, and re-layouts  0.71 us (6%)
    pallas_call x1, Pallas kernels, on_device(): pl.pallas_call(functools.partial(kernel, groups, members), out_shape=jax....  10.5 us
    unnamed x1, local copies, waits for them, and re-layouts  0.71 us

profile of v6, /device:TPU:0, one launch (start us, length us, event | category | flops | bytes accessed | tf_op | source)
XLA Modules:
  0.0 11.3 jit_solution(17228076376216831908)
XLA Ops:
  0.0 10.5 %shard_map.55 = bf16[8,32,401]{2,1,0:T(8,128)(2,1)S(1)} custom-call(f32[8,6030]{1,0:T(8,128)} %refs_0_.1, bf16[2,384,128]{2,1,0:T(8,128)(2,1)} %constant.8.clone.refs_1_, bf16[2,128,768]{2,1,0:T(8,128)(2,1)} %constant.9.clone.refs_2_, f32[24,768]{1,0:T(8,128)} %constant.10.clone.refs_3_, bf16[768,401]{1,0:T(8,128)(2,1)} %constant.11.clone.refs_4_), custom_call_target="tpu_custom_call" | custom-call | tf_op jit(solution)/shard_map/pallas_call | solution.py:257
  10.6 0.7 %copy.7 = bf16[8,32,401]{2,1,0:T(8,128)(2,1)} copy(bf16[8,32,401]{2,1,0:T(8,128)(2,1)S(1)} %shard_map.55) | data formatting | bytes 410624

commit v7 on v6

--- a/solution.py
+++ b/solution.py
@@ -90,7 +90,7 @@
         pl.semaphore_signal(barrier, inc=1, device_id=peer_of(step), device_id_type=LOGICAL)
         return carry
 
-    lax.fori_loop(1, count, greet, 0)
+    lax.fori_loop(1, count, greet, 0, unroll=count <= 32)
 
     whole = length // LANES * LANES
     padded[:, whole:] = jnp.zeros((channels, padded.shape[1] - whole), jnp.float32)
@@ -156,7 +156,7 @@
         ).start()
         return carry
 
-    lax.fori_loop(1, count, send, 0)
+    lax.fori_loop(1, count, send, 0, unroll=count <= 32)
 
     loads[4].start()
 

time: 11.4 us -> 11.4 us (level)
  no operation moved by 1% of the time
where the time goes in v7:
time: 11.4 us; the launch traced here: 11.2 us
  Pallas kernels  10.5 us (92%)
  local copies, waits for them, and re-layouts  0.71 us (6%)
    pallas_call x1, Pallas kernels, on_device(): pl.pallas_call(functools.partial(kernel, groups, members), out_shape=jax....  10.5 us
    unnamed x1, local copies, waits for them, and re-layouts  0.71 us

profile of v7, /device:TPU:0, one launch (start us, length us, event | category | flops | bytes accessed | tf_op | source)
XLA Modules:
  0.0 11.2 jit_solution(3905811680001936321)
XLA Ops:
  0.0 10.5 %shard_map.55 = bf16[8,32,401]{2,1,0:T(8,128)(2,1)S(1)} custom-call(f32[8,6030]{1,0:T(8,128)} %refs_0_.1, bf16[2,384,128]{2,1,0:T(8,128)(2,1)} %constant.8.clone.refs_1_, bf16[2,128,768]{2,1,0:T(8,128)(2,1)} %constant.9.clone.refs_2_, f32[24,768]{1,0:T(8,128)} %constant.10.clone.refs_3_, bf16[768,401]{1,0:T(8,128)(2,1)} %constant.11.clone.refs_4_), custom_call_target="tpu_custom_call" | custom-call | tf_op jit(solution)/shard_map/pallas_call | solution.py:257
  10.5 0.7 %copy.7 = bf16[8,32,401]{2,1,0:T(8,128)(2,1)} copy(bf16[8,32,401]{2,1,0:T(8,128)(2,1)S(1)} %shard_map.55) | data formatting | bytes 410624

commit v8 on v7

--- a/solution.py
+++ b/solution.py
@@ -82,9 +82,10 @@
         load.start()
     barrier = pltpu.get_barrier_semaphore()
 
+    stride = next(k for k in range(count // 4 + 1, count + 2) if math.gcd(k, count) == 1)
+
     def peer_of(step):
-        peer = me + step
-        return jnp.where(peer >= count, peer - count, peer)
+        return lax.rem(me + step * stride, count)
 
     def greet(step, carry):
         pl.semaphore_signal(barrier, inc=1, device_id=peer_of(step), device_id_type=LOGICAL)

time: 11.4 us -> 12.6 us (1.11)
  Pallas kernels: 10.5 us -> 11.7 us
    pallas_call x1, Pallas kernels: 10.5 us -> 11.7 us  [on_device(): pl.pallas_call(functools.partial(kernel, groups, members), out_shape=jax....]
where the time goes in v8:
time: 12.6 us; the launch traced here: 12.5 us
  Pallas kernels  11.7 us (93%)
  local copies, waits for them, and re-layouts  0.71 us (6%)
    pallas_call x1, Pallas kernels, on_device(): pl.pallas_call(functools.partial(kernel, groups, members), out_shape=jax....  11.7 us
    unnamed x1, local copies, waits for them, and re-layouts  0.71 us

profile of v8, /device:TPU:0, one launch (start us, length us, event | category | flops | bytes accessed | tf_op | source)
XLA Modules:
  0.0 12.5 jit_solution(14627774986040307882)
XLA Ops:
  0.0 11.7 %shard_map.55 = bf16[8,32,401]{2,1,0:T(8,128)(2,1)S(1)} custom-call(f32[8,6030]{1,0:T(8,128)} %refs_0_.1, bf16[2,384,128]{2,1,0:T(8,128)(2,1)} %constant.8.clone.refs_1_, bf16[2,128,768]{2,1,0:T(8,128)(2,1)} %constant.9.clone.refs_2_, f32[24,768]{1,0:T(8,128)} %constant.10.clone.refs_3_, bf16[768,401]{1,0:T(8,128)(2,1)} %constant.11.clone.refs_4_), custom_call_target="tpu_custom_call" | custom-call | tf_op jit(solution)/shard_map/pallas_call | solution.py:258
  11.7 0.7 %copy.7 = bf16[8,32,401]{2,1,0:T(8,128)(2,1)} copy(bf16[8,32,401]{2,1,0:T(8,128)(2,1)S(1)} %shard_map.55) | data formatting | bytes 410624

commit v9 on v8

--- a/solution.py
+++ b/solution.py
@@ -82,10 +82,13 @@
         load.start()
     barrier = pltpu.get_barrier_semaphore()
 
-    stride = next(k for k in range(count // 4 + 1, count + 2) if math.gcd(k, count) == 1)
+    bits = range(count.bit_length() - 1)
+    flips = [2**b * (1 - 2 * lax.rem(lax.div(me, 2**b), 2)) for b in bits]
 
     def peer_of(step):
-        return lax.rem(me + step * stride, count)
+        if count == 2 ** len(bits):
+            return me + sum(lax.rem(lax.div(step, 2**b), 2) * flips[b] for b in bits)
+        return lax.rem(me + step, count)
 
     def greet(step, carry):
         pl.semaphore_signal(barrier, inc=1, device_id=peer_of(step), device_id_type=LOGICAL)

time: 12.6 us -> 12.6 us (level)
  no operation moved by 1% of the time
where the time goes in v9:
time: 12.6 us; the launch traced here: 12.4 us
  Pallas kernels  11.7 us (93%)
  local copies, waits for them, and re-layouts  0.71 us (6%)
    pallas_call x1, Pallas kernels, on_device(): pl.pallas_call(functools.partial(kernel, groups, members), out_shape=jax....  11.7 us
    unnamed x1, local copies, waits for them, and re-layouts  0.71 us

profile of v9, /device:TPU:0, one launch (start us, length us, event | category | flops | bytes accessed | tf_op | source)
XLA Modules:
  0.0 12.4 jit_solution(16276042748425584577)
XLA Ops:
  0.0 11.7 %shard_map.55 = bf16[8,32,401]{2,1,0:T(8,128)(2,1)S(1)} custom-call(f32[8,6030]{1,0:T(8,128)} %refs_0_.1, bf16[2,384,128]{2,1,0:T(8,128)(2,1)} %constant.8.clone.refs_1_, bf16[2,128,768]{2,1,0:T(8,128)(2,1)} %constant.9.clone.refs_2_, f32[24,768]{1,0:T(8,128)} %constant.10.clone.refs_3_, bf16[768,401]{1,0:T(8,128)(2,1)} %constant.11.clone.refs_4_), custom_call_target="tpu_custom_call" | custom-call | tf_op jit(solution)/shard_map/pallas_call | solution.py:261
  11.7 0.7 %copy.7 = bf16[8,32,401]{2,1,0:T(8,128)(2,1)} copy(bf16[8,32,401]{2,1,0:T(8,128)(2,1)S(1)} %shard_map.55) | data formatting | bytes 410624

commit v10 on v8

--- a/solution.py
+++ b/solution.py
@@ -82,10 +82,9 @@
         load.start()
     barrier = pltpu.get_barrier_semaphore()
 
-    stride = next(k for k in range(count // 4 + 1, count + 2) if math.gcd(k, count) == 1)
-
     def peer_of(step):
-        return lax.rem(me + step * stride, count)
+        peer = me - step
+        return jnp.where(peer < 0, peer + count, peer)
 
     def greet(step, carry):
         pl.semaphore_signal(barrier, inc=1, device_id=peer_of(step), device_id_type=LOGICAL)

time: 12.6 us -> 12.7 us (level)
  no operation moved by 1% of the time
where the time goes in v10:
time: 12.7 us; the launch traced here: 12.5 us
  Pallas kernels  11.8 us (93%)
  local copies, waits for them, and re-layouts  0.71 us (6%)
    pallas_call x1, Pallas kernels, on_device(): pl.pallas_call(functools.partial(kernel, groups, members), out_shape=jax....  11.8 us
    unnamed x1, local copies, waits for them, and re-layouts  0.71 us

profile of v10, /device:TPU:0, one launch (start us, length us, event | category | flops | bytes accessed | tf_op | source)
XLA Modules:
  0.0 12.5 jit_solution(7340409394314266036)
XLA Ops:
  0.0 11.8 %shard_map.55 = bf16[8,32,401]{2,1,0:T(8,128)(2,1)S(1)} custom-call(f32[8,6030]{1,0:T(8,128)} %refs_0_.1, bf16[2,384,128]{2,1,0:T(8,128)(2,1)} %constant.8.clone.refs_1_, bf16[2,128,768]{2,1,0:T(8,128)(2,1)} %constant.9.clone.refs_2_, f32[24,768]{1,0:T(8,128)} %constant.10.clone.refs_3_, bf16[768,401]{1,0:T(8,128)(2,1)} %constant.11.clone.refs_4_), custom_call_target="tpu_custom_call" | custom-call | tf_op jit(solution)/shard_map/pallas_call | solution.py:257
  11.8 0.7 %copy.7 = bf16[8,32,401]{2,1,0:T(8,128)(2,1)} copy(bf16[8,32,401]{2,1,0:T(8,128)(2,1)S(1)} %shard_map.55) | data formatting | bytes 410624
